TPU v7x, 256 devices: a whole 4x4x8 slice. The times are simulated.
256 devices in a mesh: group: 4 (over x_lo, core), fsdp: 64 (over z, x_hi, y).
Axes of the slice: x: 4 (x_hi: 2, x_lo: 2; x = x_hi * 2 + x_lo), y: 4, z: 8, core: 2. Of those that a mesh axis runs over, the one named last changes fastest.
Arguments:
- tokens: bfloat16 [4, 128, 7168], P('group', 'fsdp'), may hold values from -6 to 6
- target: float32 [4, 128, 7168], P('group', 'fsdp'), may hold values from -6 to 6
- up_weight: bfloat16 [4, 10240, 7168], P('group', 'fsdp'), may hold values from -6 to 6
- down_weight: bfloat16 [4, 10240, 7168], P('group', 'fsdp'), may hold values from -6 to 6
Outputs:
- student_out: bfloat16 [4, 128, 7168], P('group', 'fsdp')
- new_up: bfloat16 [4, 10240, 7168], P('group', 'fsdp')
- new_down: bfloat16 [4, 10240, 7168], P('group', 'fsdp')
All inputs are finite; a program needn't handle non-finite values.
Results may differ from a plain program's by a relative error of at most 0.0065.
Values may be sent and summed in bfloat16 or wider, within the bound.
A program may use at most 128 MiB of HBM per device.

v0:
```python
import math

import jax
import jax.numpy as jnp
from jax import lax
from jax.sharding import PartitionSpec as P

FFW = 10240


def from_behind(shard, axis, by):
    count = lax.axis_size(axis)
    return lax.ppermute(shard, axis, [(i, (i + by) % count) for i in range(count)])


def silu_parts(pre):
    sig = jax.nn.sigmoid(pre)
    return (pre * sig, sig * (1.0 + pre * (1.0 - sig)))


def hidden_of(inputs, upper):
    width = upper.shape[1]
    pre = lax.dot_general(
        inputs, upper, (((1,), (1,)), ((), ())), preferred_element_type=jnp.float32
    ) * (1.0 / math.sqrt(width))
    active, slope = silu_parts(pre)
    return (active.astype(jnp.bfloat16), slope)


def teacher_share(hidden, lower):
    return lax.psum_scatter(
        jnp.dot(hidden, lower, preferred_element_type=jnp.float32) * (1.0 / math.sqrt(FFW)),
        "fsdp",
        scatter_dimension=0,
        tiled=True,
    )


def shards(tokens, target, up_weight, down_weight):
    inputs = tokens[0]
    goal = target[0]
    upper = up_weight[0]
    lower = down_weight[0]
    width = upper.shape[1]
    gathered = lax.all_gather(inputs, "fsdp", axis=0, tiled=True)
    total_rows = gathered.shape[0]
    hidden, slope = hidden_of(gathered, upper)
    student = lax.psum_scatter(
        jnp.dot(hidden, lower, preferred_element_type=jnp.float32) * (1.0 / math.sqrt(FFW)),
        "fsdp",
        scatter_dimension=0,
        tiled=True,
    )
    stale_up, stale_down = from_behind((upper, lower), "group", 1)
    teacher_hidden, unused_slope = hidden_of(gathered, stale_up)
    teacher = teacher_share(teacher_hidden, stale_down)
    error = ((student - goal + (student - teacher)) * (1.0 / math.sqrt(total_rows))).astype(
        jnp.bfloat16
    )
    error_all = lax.all_gather(error, "fsdp", axis=0, tiled=True)
    grad_down = lax.dot_general(
        hidden, error_all, (((0,), (0,)), ((), ())), preferred_element_type=jnp.float32
    ) * (1.0 / math.sqrt(FFW))
    back = lax.dot_general(
        error_all, lower, (((1,), (1,)), ((), ())), preferred_element_type=jnp.float32
    ) * (1.0 / math.sqrt(FFW))
    dpre = (back * slope).astype(jnp.bfloat16)
    grad_up = lax.dot_general(
        dpre, gathered, (((0,), (0,)), ((), ())), preferred_element_type=jnp.float32
    ) * (1.0 / math.sqrt(width))
    new_upper = (upper.astype(jnp.float32) - 32.0 * grad_up).astype(jnp.bfloat16)
    new_lower = (lower.astype(jnp.float32) - 32.0 * grad_down).astype(jnp.bfloat16)
    return (student.astype(jnp.bfloat16)[None], new_upper[None], new_lower[None])


def solution(mesh):
    placed = (
        P("group", "fsdp", None),
        P("group", "fsdp", None),
        P("group", "fsdp", None),
        P("group", "fsdp", None),
    )
    return jax.shard_map(
        shards,
        mesh=mesh,
        in_specs=placed,
        out_specs=(P("group", "fsdp", None), P("group", "fsdp", None), P("group", "fsdp", None)),
        check_vma=False,
    )
```

profile of v0, /device:TPU:16, one launch (start us, length us, event | category | flops | bytes accessed | tf_op | source)
XLA Modules:
  0.0 1015.1 jit_solution(2403152746552988402)
XLA Ops:
  7.2 0.0 copy-start
  7.2 0.0 all-gather.5.cloned.1.call-start
  7.2 1.6 copy.8
  8.8 0.0 all-gather.5.cloned.1.call-update
  8.8 0.0 all-reduce.5.cloned.1.call-start
  8.9 0.1 collective-permute-start
  9.0 1.6 collective-permute-start.1
  10.5 130.6 %all-gather.5.cloned.1.call-done = bf16[1,128,7168]{2,0,1:T(2,128)(2,1)} async-done(((bf16[1,2,7168]{2,0,1:T(2,128)(2,1)}), bf16[1,128,7168]{2,0,1:T(2,128)(2,1)}) %all-gather.5.cloned.1.call-update) | async-done | bytes 1835024 | tf_op jit(solution)/shard_map/all_gather | solution.py:45
  141.1 3.6 fusion.11
  144.8 0.0 copy-done
  144.8 2.5 convolution_multiply_fusion.3
  147.3 0.0 collective-permute-done
  147.3 0.0 collective-permute-done.1
  147.3 7.7 convolution_multiply_fusion.2
  155.0 0.0 copy-start.2
  155.0 0.0 copy-start.1
  155.0 0.0 all-reduce.5.cloned.1.call-update
  155.0 0.0 all-gather.7.cloned.1.call-start
  155.1 0.6 copy-done.2
  155.7 0.6 dynamic-slice
  156.9 714.8 %all-reduce.5.cloned.1.call-done = (f32[128,7168]{1,0:T(8,128)}, f32[128,7168]{1,0:T(8,128)}) async-done(((f32[128,7168]{1,0:T(8,128)}, f32[128,7168]{1,0:T(8,128)}), (f32[128,7168]{1,0:T(8,128)}, f32[128,7168]{1,0:T(8,128)})) %all-reduce.5.cloned.1.call-update) | async-done | bytes 7340048
  871.7 0.0 copy-done.1
  871.7 1.7 fusion.35
  873.4 0.0 all-gather.7.cloned.1.call-update
  873.5 1.6 fusion.34
  875.1 117.7 %all-gather.7.cloned.1.call-done = bf16[64,2,7168]{2,1,0:T(2,128)(2,1)} async-done(((bf16[1,2,7168]{2,1,0:T(2,128)(2,1)}), bf16[64,2,7168]{2,1,0:T(2,128)(2,1)}) %all-gather.7.cloned.1.call-update) | async-done | bytes 1835024 | tf_op jit(solution)/shard_map/all_gather | solution.py:60
  992.7 4.9 reshape.8
  997.6 3.6 fusion.4
  1001.3 7.3 fusion.5
Async XLA Ops:
  7.2 137.6 %copy-start = (bf16[1,160,7168]{2,1,0:T(8,128)(2,1)S(1)}, bf16[1,160,7168]{2,1,0:T(8,128)(2,1)}, u32[]{:S(2)}) copy-start(bf16[1,160,7168]{2,1,0:T(8,128)(2,1)} %param.7) | copy-start | bytes 6881284
  7.2 134.0 %all-gather.5.cloned.1.call-start = ((), (), s32[]{:S(2)}) async-start(), calls=%async_computation | async-start | bytes 3727360 | tf_op jit(solution)/shard_map/all_gather | solution.py:45
  8.8 862.9 %all-reduce.5.cloned.1.call-start = ((), (), s32[]{:S(2)}) async-start(), calls=%async_computation.2 | async-start | bytes 14680064
  8.9 138.4 %collective-permute-start = (bf16[160,7168]{1,0:T(8,128)(2,1)}, bf16[160,7168]{1,0:T(8,128)(2,1)}, u32[]{:S(2)}, u32[]{:S(2)}) collective-permute-start(bf16[160,7168]{1,0:T(8,128)(2,1)} %bitcast.48), channel_id=1, source_target_pairs={{0,64},{64,128},{128,192},{192,0},{1,65},{65,129},{129,193},{193,1... | collective-permute-start | bytes 6881288 | tf_op jit(solution)/shard_map/ppermute | solution.py:13
  9.0 138.3 %collective-permute-start.1 = (bf16[160,7168]{1,0:T(8,128)(2,1)}, bf16[160,7168]{1,0:T(8,128)(2,1)}, u32[]{:S(2)}, u32[]{:S(2)}) collective-permute-start(bf16[160,7168]{1,0:T(8,128)(2,1)} %bitcast.47), channel_id=1, source_target_pairs={{0,64},{64,128},{128,192},{192,0},{1,65},{65,129},{129,193},{193,1... | collective-permute-start | bytes 6881288 | tf_op jit(solution)/shard_map/ppermute | solution.py:13
  155.0 0.7 copy-start.2
  155.0 716.7 %copy-start.1 = (f32[1,2,7168]{2,1,0:T(2,128)S(1)}, f32[1,2,7168]{2,1,0:T(2,128)}, u32[]{:S(2)}) copy-start(f32[1,2,7168]{2,1,0:T(2,128)} %param.5) | copy-start | bytes 172036
  155.0 837.7 %all-gather.7.cloned.1.call-start = ((), (), s32[]{:S(2)}) async-start(), calls=%async_computation.1 | async-start | bytes 1863680 | tf_op jit(solution)/shard_map/all_gather | solution.py:60
Sparse Core Ops, SparseCore 0:
  12.3 128.8 all-gather.4
  155.1 716.5 all-reduce.4
  876.3 116.3 all-gather.6
where the time goes:
time: 1020 us
  waiting for transfers between devices  963 us (94%)
  matrix products  24.8 us (2%)
  between operations  14.4 us (1%)
    unnamed x4, waiting for transfers between devices  715 us
    all_gather x1, waiting for transfers between devices, shards(): gathered = lax.all_gather(inputs, 'fsdp', axis=0, tiled=True)  131 us
    all_gather x1, waiting for transfers between devices, shards(): error_all = lax.all_gather(error, 'fsdp', axis=0, tiled=True)  118 us
  transfers between devices with their start and end apart: 5, of which 3 were waited for; matrix products, arithmetic and copies ran while one was open for 1% of the time, Pallas kernels for 0%

commit v1 on v0

v1 whole, which is shorter than its diff:
```python
import functools
import math

import jax
import jax.numpy as jnp
from jax import lax
from jax.experimental import pallas as pl
from jax.experimental.pallas import tpu as pltpu
from jax.sharding import PartitionSpec as P

MESH = pl.DeviceIdType.MESH
F32, BF16 = jnp.float32, jnp.bfloat16
D, FFW, TOKENS, HID = 7168, 10240, 128, 160
NZ, NP, ROWS = 8, 8, 16
HALF = D // 2
CHUNK = 1792
NCHUNK = D // CHUNK
UP_SCALE = 1.0 / math.sqrt(D)
DOWN_SCALE = 1.0 / math.sqrt(FFW)


def half(h):
    return pl.ds(h * HALF, HALF)


def kernel(
    tok, tgt, up_hbm, down_hbm, stu, nup_hbm, ndown_hbm,
    U, W, X, T, P1, P2, E, R, PB, EGB, EB, SB, RB, STK, load_sem, store_sem,
    pg_send, pg_recv, zg_send, zg_recv, tf_send, tf_recv,
    rs_send, rs_recv, pr_send, pr_recv, eg_send, eg_recv, ze_send, ze_recv,
):
    g = lax.axis_index("group")
    f = lax.axis_index("fsdp")
    z = f // NP
    me = f % NP
    base = z * NP
    below = (g + 3) % 4
    above = (g + 1) % 4
    up_z = ((z + 1) % NZ) * NP + me
    down_z = ((z + NZ - 1) % NZ) * NP + me
    ring = (up_z, down_z)
    flip = base + (me + 4) % NP
    other = jnp.where(g % 2 == 1, f, flip)

    load_up = pltpu.make_async_copy(up_hbm, U, load_sem.at[0])
    load_down = pltpu.make_async_copy(down_hbm, W, load_sem.at[1])
    load_up.start()
    load_down.start()

    barrier = pltpu.get_barrier_semaphore()
    for r in range(1, NP):
        pl.semaphore_signal(barrier, inc=1, device_id=(g, base + (me + r) % NP), device_id_type=MESH)
    for r in range(NP):
        pl.semaphore_signal(barrier, inc=1, device_id=(above, base + (me + r) % NP), device_id_type=MESH)
        pl.semaphore_signal(barrier, inc=1, device_id=(below, base + (me + r) % NP), device_id_type=MESH)
    for d in range(2):
        pl.semaphore_signal(barrier, inc=1, device_id=(g, ring[d]), device_id_type=MESH)
    pl.semaphore_wait(barrier, 3 * NP - 1 + 2)

    pending = []

    def plane_gather(src, buf, send, recv, slab):
        copies = []
        for r in range(1, NP):
            c = pltpu.make_async_remote_copy(
                src_ref=src, dst_ref=buf.at[me], send_sem=send.at[r], recv_sem=recv.at[r],
                device_id=(g, base + (me + r) % NP), device_id_type=MESH)
            c.start()
            copies.append(c)
        for c in copies:
            c.wait_recv()
        buf[me] = src[...]
        for j in range(NP):
            STK[2 * j:2 * j + 2, :] = buf[j].astype(F32)
        slab[...] = STK[...].astype(BF16)
        pending.extend(copies)

    def ring_gather(buf, send, recv, forward=None):
        def send_slab(d, s, h):
            slab = (z + s) % NZ if d == 1 else (z + NZ - s) % NZ
            c = pltpu.make_async_remote_copy(
                src_ref=buf.at[slab, :, half(h)], dst_ref=buf.at[slab, :, half(h)],
                send_sem=send.at[d, s, h], recv_sem=recv.at[d, s, h],
                device_id=(g, ring[d]), device_id_type=MESH)
            c.start()
            pending.append(c)
            return c

        flight = {}
        for h in range(2):
            for d in range(2):
                flight[d, 0, h] = send_slab(d, 0, h)
        if forward is not None:
            forward(z, 0, 0)
            forward(z, 0, 1)
        for s in range(1, 5):
            for h in range(2):
                for d in range(2):
                    if (d, s - 1, h) not in flight:
                        continue
                    flight[d, s - 1, h].wait_recv()
                    if s < 3 or (s == 3 and h == d):
                        flight[d, s, h] = send_slab(d, s, h)
                    if forward is not None:
                        got = (z + s) % NZ if d == 1 else (z + NZ - s) % NZ
                        forward(got, s if d == 0 else (s + 4 if s < 4 else 4), h)

    sent_t = []

    def forward(slab, slot, h):
        dev = f if h == 0 else other
        c = pltpu.make_async_remote_copy(
            src_ref=X.at[slab, :, half(h)], dst_ref=T.at[slab, :, half(h)],
            send_sem=tf_send.at[slot, h], recv_sem=tf_recv.at[slot, h],
            device_id=(below, dev), device_id_type=MESH)
        c.start()
        sent_t.append(c)

    plane_gather(tok, PB, pg_send, pg_recv, X.at[z])
    ring_gather(X, zg_send, zg_recv, forward)

    load_up.wait()
    load_down.wait()

    def pre_of(A):
        def body(i, acc):
            cols = pl.ds(pl.multiple_of(i * CHUNK, CHUNK), CHUNK)
            a = A[:, :, cols].reshape(TOKENS, CHUNK)
            return acc + lax.dot_general(
                a, U[:, cols], (((1,), (1,)), ((), ())), preferred_element_type=F32)
        return lax.fori_loop(0, NCHUNK, body, jnp.zeros((TOKENS, HID), F32)) * UP_SCALE

    def partial_out(hidden, out):
        def body(i, _):
            cols = pl.ds(pl.multiple_of(i * CHUNK, CHUNK), CHUNK)
            v = jnp.dot(hidden, W[:, cols], preferred_element_type=F32) * DOWN_SCALE
            out[:, :, cols] = v.astype(BF16).reshape(NZ, ROWS, CHUNK)
            return 0
        lax.fori_loop(0, NCHUNK, body, 0)

    rflight = {}

    def rs_start(w, part):
        for d in range(2):
            c = pltpu.make_async_remote_copy(
                src_ref=part.at[(z + 4) % NZ, :, half(d)], dst_ref=R.at[w, d, 0, :, half(d)],
                send_sem=rs_send.at[w, d, 0, d], recv_sem=rs_recv.at[w, d, 0, d],
                device_id=(g, ring[d]), device_id_type=MESH)
            c.start()
            rflight[w, d, 0, d] = c
        for d in range(2):
            dest = (z + 3) % NZ if d == 0 else (z + NZ - 3) % NZ
            h = 1 - d
            c = pltpu.make_async_remote_copy(
                src_ref=part.at[dest, :, half(h)], dst_ref=R.at[w, d, 1, :, half(h)],
                send_sem=rs_send.at[w, d, 1, h], recv_sem=rs_recv.at[w, d, 1, h],
                device_id=(g, ring[d]), device_id_type=MESH)
            c.start()
            rflight[w, d, 1, h] = c

    def rs_step(w, part, s):
        for h in range(2):
            for d in range(2):
                if (w, d, s - 1, h) not in rflight:
                    continue
                rflight[w, d, s - 1, h].wait_recv()
                dest = (z + 4 - s) % NZ if d == 0 else (z + NZ - 4 + s) % NZ
                cols = half(h)
                R[w, d, s - 1, :, cols] = (
                    R[w, d, s - 1, :, cols].astype(F32) + part[dest, :, cols].astype(F32)
                ).astype(BF16)
                c = pltpu.make_async_remote_copy(
                    src_ref=R.at[w, d, s - 1, :, cols], dst_ref=R.at[w, d, s, :, cols],
                    send_sem=rs_send.at[w, d, s, h], recv_sem=rs_recv.at[w, d, s, h],
                    device_id=(g, ring[d]), device_id_type=MESH)
                c.start()
                rflight[w, d, s, h] = c

    pr = []

    def rs_finish(w, part):
        for h in range(2):
            for d in range(2):
                rflight[w, d, 3, h].wait_recv()
        total = part[z].astype(F32) + R[w, 0, 3].astype(F32) + R[w, 1, 3].astype(F32)
        STK[...] = total
        for j in range(NP):
            SB[w, j] = STK[2 * j:2 * j + 2, :].astype(BF16)
        for r in range(NP):
            if w == 0 and r == 0:
                continue
            peer = (me + r) % NP
            c = pltpu.make_async_remote_copy(
                src_ref=SB.at[w, peer], dst_ref=RB.at[w, me],
                send_sem=pr_send.at[w, r], recv_sem=pr_recv.at[w, r],
                device_id=(g if w == 0 else above, base + peer), device_id_type=MESH)
            c.start()
            pr.append(c)
        if w == 0:
            RB[w, me] = SB[w, me]

    pre = pre_of(X)
    sig = jax.nn.sigmoid(pre)
    hidden = (pre * sig).astype(BF16)
    slope = sig * (1.0 + pre * (1.0 - sig))
    partial_out(hidden, P1)
    rs_start(0, P1)
    for c in sent_t:
        c.wait_recv()
    pre_t = pre_of(T)
    hidden_t = (pre_t * jax.nn.sigmoid(pre_t)).astype(BF16)
    partial_out(hidden_t, P2)
    rs_start(1, P2)
    parts = (P1, P2)
    for s in range(1, 4):
        for w in range(2):
            rs_step(w, parts[w], s)
    for w in range(2):
        rs_finish(w, parts[w])
    for c in pr:
        c.wait_recv()
    ys = jnp.sum(RB[0].astype(F32), axis=0)
    yt = jnp.sum(RB[1].astype(F32), axis=0)
    stu[...] = ys.astype(BF16)
    EB[...] = ((ys - tgt[...] + (ys - yt)) * (1.0 / math.sqrt(TOKENS))).astype(BF16)

    plane_gather(EB, EGB, eg_send, eg_recv, E.at[z])
    ring_gather(E, ze_send, ze_recv)

    hidden_t_up = jnp.transpose(hidden.astype(F32)).astype(BF16)

    def back_body(i, acc):
        cols = pl.ds(pl.multiple_of(i * CHUNK, CHUNK), CHUNK)
        e = E[:, :, cols].reshape(TOKENS, CHUNK)
        w = W[:, cols]
        acc = acc + lax.dot_general(
            e, w, (((1,), (1,)), ((), ())), preferred_element_type=F32)
        grad = jnp.dot(hidden_t_up, e, preferred_element_type=F32) * DOWN_SCALE
        W[:, cols] = (w.astype(F32) - 32.0 * grad).astype(BF16)
        return acc

    back = lax.fori_loop(0, NCHUNK, back_body, jnp.zeros((TOKENS, HID), F32)) * DOWN_SCALE
    store_down = pltpu.make_async_copy(W, ndown_hbm, store_sem.at[0])
    store_down.start()
    dpre_t = jnp.transpose(back * slope).astype(BF16)

    def up_body(i, _):
        cols = pl.ds(pl.multiple_of(i * CHUNK, CHUNK), CHUNK)
        x = X[:, :, cols].reshape(TOKENS, CHUNK)
        grad = jnp.dot(dpre_t, x, preferred_element_type=F32) * UP_SCALE
        U[:, cols] = (U[:, cols].astype(F32) - 32.0 * grad).astype(BF16)
        return 0

    lax.fori_loop(0, NCHUNK, up_body, 0)
    store_up = pltpu.make_async_copy(U, nup_hbm, store_sem.at[1])
    store_up.start()
    for c in pending + sent_t + pr + list(rflight.values()):
        c.wait_send()
    store_down.wait()
    store_up.wait()


def shards(tokens, target, up_weight, down_weight):
    anywhere = pl.BlockSpec(memory_space=pl.ANY)
    vmem = pl.BlockSpec(memory_space=pltpu.VMEM)
    dma = pltpu.SemaphoreType.DMA
    student, new_up, new_down = pl.pallas_call(
        kernel,
        out_shape=(
            jax.ShapeDtypeStruct((2, D), BF16),
            jax.ShapeDtypeStruct((HID, D), BF16),
            jax.ShapeDtypeStruct((HID, D), BF16),
        ),
        in_specs=[vmem, vmem, anywhere, anywhere],
        out_specs=(vmem, anywhere, anywhere),
        scratch_shapes=[
            pltpu.VMEM((HID, D), BF16),
            pltpu.VMEM((HID, D), BF16),
            pltpu.VMEM((NZ, ROWS, D), BF16),
            pltpu.VMEM((NZ, ROWS, D), BF16),
            pltpu.VMEM((NZ, ROWS, D), BF16),
            pltpu.VMEM((NZ, ROWS, D), BF16),
            pltpu.VMEM((NZ, ROWS, D), BF16),
            pltpu.VMEM((2, 2, 4, ROWS, D), BF16),
            pltpu.VMEM((NP, 2, D), BF16),
            pltpu.VMEM((NP, 2, D), BF16),
            pltpu.VMEM((2, D), BF16),
            pltpu.VMEM((2, NP, 2, D), BF16),
            pltpu.VMEM((2, NP, 2, D), BF16),
            pltpu.VMEM((ROWS, D), F32),
            dma((2,)), dma((2,)),
            dma((NP,)), dma((NP,)),
            dma((2, 4, 2)), dma((2, 4, 2)),
            dma((8, 2)), dma((8, 2)),
            dma((2, 2, 4, 2)), dma((2, 2, 4, 2)),
            dma((2, NP)), dma((2, NP)),
            dma((NP,)), dma((NP,)),
            dma((2, 4, 2)), dma((2, 4, 2)),
        ],
        compiler_params=pltpu.CompilerParams(
            collective_id=0, has_side_effects=True, vmem_limit_bytes=48 * 1024 * 1024),
        cost_estimate=pl.CostEstimate(
            flops=14 * TOKENS * HID * D, bytes_accessed=8 * HID * D, transcendentals=2 * TOKENS * HID),
        name="codistill",
    )(tokens[0], target[0], up_weight[0], down_weight[0])
    return student[None], new_up[None], new_down[None]


def solution(mesh):
    placed = P("group", "fsdp", None)
    return jax.shard_map(
        shards, mesh=mesh, in_specs=(placed,) * 4, out_specs=(placed,) * 3, check_vma=False)
```

time: 1020 us -> 121 us (0.12)
  waiting for transfers between devices: 963 us -> 0 us
  Pallas kernels: 0 us -> 115 us
  matrix products: 24.8 us -> 0 us
  between operations: 14.4 us -> 0.65 us
    unnamed x4 -> x0, waiting for transfers between devices: 715 us -> none
    all_gather x2 -> x0, waiting for transfers between devices: 248 us -> none  [the longest x1 131 us: shards(): gathered = lax.all_gather(inputs, 'fsdp', axis=0, tiled=True)]
    pallas_call x0 -> x1, Pallas kernels: none -> 115 us  [shards(): pl.pallas_call(kernel, out_shape=(jax.ShapeDtypeStruct((2, D), BF16), jax...]
    dot_general x5 -> x0, matrix products: 24.8 us -> none  [the longest x1 7.69 us: teacher_share(): jnp.dot(hidden, lower, preferred_element_type=jnp.float32)]
  transfers between devices with their start and end apart: 5 -> 0, of which waited for: 3 -> 0; matrix products, arithmetic and copies ran while one was open for 1% -> 0% of each run, Pallas kernels for 0% -> 0%
where the time goes in v1:
time: 121 us; the launch traced here: 120 us
  Pallas kernels  115 us (95%)
  local copies, waits for them, and re-layouts  4.94 us (4%)
    pallas_call x1, Pallas kernels, shards(): pl.pallas_call(kernel, out_shape=(jax.ShapeDtypeStruct((2, D), BF16), jax...  115 us
    unnamed x7, local copies, waits for them, and re-layouts  4.94 us

profile of v1, /device:TPU:16, one launch (start us, length us, event | category | flops | bytes accessed | tf_op | source)
XLA Modules:
  0.0 120.3 jit_solution(5375170813556788326)
XLA Ops:
  0.6 0.0 copy-start
  0.6 0.8 copy-done
  1.5 0.0 copy-start.1
  1.5 0.7 copy-done.1
  2.2 114.8 %codistill.1 = (bf16[2,7168]{1,0:T(2,128)(2,1)S(1)}, bf16[160,7168]{1,0:T(8,128)(2,1)S(1)}, bf16[160,7168]{1,0:T(8,128)(2,1)S(1)}) custom-call(bf16[2,7168]{1,0:T(2,128)(2,1)S(1)} %bitcast.11, f32[2,7168]{1,0:T(2,128)S(1)} %bitcast.10, bf16[160,7168]{1,0:T(8,128)(2,1)} %bitcast.12, bf16[160,7168]{1,0:T(8,128)(2,1)} %bitcast.13), custom_call_target="tpu_custom_call" | custom-call | flops 2055208960 | bytes 9175040 | tf_op jit(solution)/shard_map/codistill/pallas_call | solution.py:267
  117.0 0.6 copy.10
  117.6 1.4 %copy.11 = bf16[1,160,7168]{2,1,0:T(8,128)(2,1)} copy(bf16[1,160,7168]{2,1,0:T(8,128)(2,1)S(1)} %bitcast.8) | data formatting | bytes 4587520
  119.0 1.4 %copy.12 = bf16[1,160,7168]{2,1,0:T(8,128)(2,1)} copy(bf16[1,160,7168]{2,1,0:T(8,128)(2,1)S(1)} %bitcast.7) | data formatting | bytes 4587520
Async XLA Ops:
  0.6 0.8 copy-start
  1.5 0.7 copy-start.1

commit v2 on v0

v2 whole, which is shorter than its diff:
```python
import math

import jax
import jax.numpy as jnp
from jax import lax
from jax.experimental import pallas as pl
from jax.experimental.pallas import tpu as pltpu
from jax.sharding import PartitionSpec as P

MESH = pl.DeviceIdType.MESH
F32, BF16 = jnp.float32, jnp.bfloat16
D, FFW, TOKENS, HID = 7168, 10240, 128, 160
NZ, NP, NY, ROWS = 8, 8, 4, 16
CA = 3072
CB = D - CA
HA, HB = CA // 2, CB // 2
UP_SCALE = 1.0 / math.sqrt(D)
DOWN_SCALE = 1.0 / math.sqrt(FFW)

SCRATCH = {}


def scratch(name, shape, kind=BF16):
    SCRATCH[name] = pltpu.SemaphoreType.DMA(shape) if kind is None else pltpu.VMEM(shape, kind)


scratch("tok", (2, D))
scratch("tgt", (2, D), F32)
scratch("U", (HID, D))
scratch("W", (HID, D))
for n in ("X", "T", "P1", "P2", "E"):
    scratch(n + "a", (NZ, ROWS, CA))
    scratch(n + "b", (NP, ROWS, CB))
scratch("RA", (2, 2, 4, ROWS, CA))
scratch("RY", (2, 2, 2, 2, ROWS, CB))
scratch("XS", (2, ROWS, CB))
scratch("XR", (2, ROWS, CB))
scratch("err", (2, D))
for n in ("G1", "G2"):
    scratch(n + "a", (NP, 2, CA))
    scratch(n + "b", (NZ, 2, CB))
for n in ("S", "R"):
    scratch(n + "Pa", (2, NP, 2, CA))
    scratch(n + "Pb", (2, NZ, 2, CB))
scratch("STKa", (ROWS, CA), F32)
scratch("STKb", (ROWS, CB), F32)
scratch("load", (4,), None)
scratch("store", (2,), None)
for n in ("g1", "g2"):
    for e in ("s", "r"):
        scratch(n + "pa" + e, (NP,), None)
        scratch(n + "pb" + e, (NZ,), None)
        scratch(n + "za" + e, (2, 4, 2), None)
        scratch(n + "xb" + e, (2,), None)
        scratch(n + "yb" + e, (2, 2, 2, 2), None)
for e in ("s", "r"):
    scratch("ta" + e, (NZ, 2), None)
    scratch("tb" + e, (NP, 2), None)
    scratch("ra" + e, (2, 2, 4, 2), None)
    scratch("ry" + e, (2, 2, 2, 2, 2), None)
    scratch("rx" + e, (2, 2), None)
    scratch("pa" + e, (2, NP), None)
    scratch("pb" + e, (2, NZ), None)


def kernel(tok_hbm, tgt_hbm, up_hbm, down_hbm, stu, nup_hbm, ndown_hbm, *refs):
    v = dict(zip(SCRATCH, refs))
    tok, U, W = v["tok"], v["U"], v["W"]
    g = lax.axis_index("group")
    f = lax.axis_index("fsdp")
    z = f // NP
    me = f % NP
    xh = me // NY
    yy = me % NY
    base = z * NP
    below = (g + 3) % 4
    above = (g + 1) % 4
    zring = (((z + 1) % NZ) * NP + me, ((z + NZ - 1) % NZ) * NP + me)
    yring = (base + xh * NY + (yy + 1) % NY, base + xh * NY + (yy + NY - 1) % NY)
    flip = base + (me + 4) % NP
    other = jnp.where(g % 2 == 1, f, flip)

    def colsa(h):
        return pl.ds(h * HA, HA)

    def colsb(h):
        return pl.ds(h * HB, HB)

    loads = [
        pltpu.make_async_copy(src, dst, v["load"].at[i])
        for i, (src, dst) in enumerate(
            ((tok_hbm, tok), (up_hbm, U), (down_hbm, W), (tgt_hbm, v["tgt"])))
    ]
    for c in loads:
        c.start()

    barrier = pltpu.get_barrier_semaphore()
    peers = [(g, base + (me + r) % NP) for r in range(1, NP)]
    peers += [(g, ((z + r) % NZ) * NP + me) for r in range(1, NZ)]
    peers += [(above, f), (above, flip), (below, f), (below, flip)]
    for p in peers:
        pl.semaphore_signal(barrier, inc=1, device_id=p, device_id_type=MESH)
    pl.semaphore_wait(barrier, len(peers))

    started = []

    def send(src, dst, sems, at, dev):
        c = pltpu.make_async_remote_copy(
            src_ref=src, dst_ref=dst, send_sem=v[sems + "s"].at[at], recv_sem=v[sems + "r"].at[at],
            device_id=dev, device_id_type=MESH)
        c.start()
        started.append(c)
        return c

    def slab_of(p, k, s):
        x = xh if k == 0 else 1 - xh
        return x * NY + (yy + s + NY) % NY

    def stack(buf, stk, slab):
        for j in range(8):
            stk[2 * j:2 * j + 2, :] = buf[j].astype(F32)
        slab[...] = stk[...].astype(BF16)

    def gather(src, n, name, forward):
        Ga, Gb = v[n.upper() + "a"], v[n.upper() + "b"]
        A, B = v[name + "a"], v[name + "b"]
        first_a = [
            send(src.at[:, pl.ds(0, CA)], Ga.at[me], n + "pa", (r,), (g, base + (me + r) % NP))
            for r in range(1, NP)]
        first_b = [
            send(src.at[:, pl.ds(CA, CB)], Gb.at[z], n + "pb", (r,), (g, ((z + r) % NZ) * NP + me))
            for r in range(1, NZ)]
        Ga[me] = src[:, 0:CA]
        Gb[z] = src[:, CA:D]
        fly = {}

        def send_a(d, s, h):
            at = (z + s) % NZ if d == 1 else (z + NZ - s) % NZ
            ref = A.at[at, :, colsa(h)]
            fly["a", d, s, h] = send(ref, ref, n + "za", (d, s, h), (g, zring[d]))

        def step_a(s):
            for h in range(2):
                for d in range(2):
                    if ("a", d, s - 1, h) not in fly:
                        continue
                    fly["a", d, s - 1, h].wait_recv()
                    if s < 3 or (s == 3 and h == d):
                        send_a(d, s, h)
                    if forward:
                        at = (z + s) % NZ if d == 1 else (z + NZ - s) % NZ
                        forward("a", at, s if d == 0 else (s + 4 if s < 4 else 4), h)

        def send_b(d, k, s, h):
            at = slab_of(me, k, s if d == 1 else -s)
            ref = B.at[at, :, colsb(h)]
            fly["b", d, k, s, h] = send(ref, ref, n + "yb", (d, k, s, h), (g, yring[d]))

        def step_b(k, s):
            for h in range(2):
                for d in range(2):
                    if ("b", d, k, s - 1, h) not in fly:
                        continue
                    fly["b", d, k, s - 1, h].wait_recv()
                    if s == 1 and h == d:
                        send_b(d, k, 1, h)
                    if forward:
                        at = slab_of(me, k, s if d == 1 else -s)
                        slot = 4 * k + (s if d == 0 else (3 if s == 1 else 2))
                        forward("b", at, slot, h)

        for c in first_a:
            c.wait_recv()
        stack(Ga, v["STKa"], A.at[z])
        for h in range(2):
            for d in range(2):
                send_a(d, 0, h)
        for c in first_b:
            c.wait_recv()
        stack(Gb, v["STKb"], B.at[me])
        for h in range(2):
            ref = B.at[me, :, colsb(h)]
            fly["x", h] = send(ref, ref, n + "xb", (h,), (g, flip))
            for d in range(2):
                send_b(d, 0, 0, h)
        if forward:
            for h in range(2):
                forward("a", z, 0, h)
                forward("b", me, 0, h)
        step_a(1)
        for h in range(2):
            fly["x", h].wait_recv()
            for d in range(2):
                send_b(d, 1, 0, h)
            if forward:
                forward("b", slab_of(me, 1, 0), 4, h)
        step_b(0, 1)
        step_a(2)
        step_b(1, 1)
        step_a(3)
        step_b(0, 2)
        step_a(4)
        step_b(1, 2)

    sent_t = []

    def forward(o, slab, slot, h):
        cols = colsa(h) if o == "a" else colsb(h)
        sent_t.append(send(
            v["X" + o].at[slab, :, cols], v["T" + o].at[slab, :, cols], "t" + o, (slot, h),
            (below, f if h == 0 else other)))

    loads[0].wait()
    gather(tok, "g1", "X", forward)
    loads[1].wait()
    loads[2].wait()
    loads[3].wait()

    row = lax.broadcasted_iota(jnp.int32, (TOKENS, TOKENS), 0)
    col = lax.broadcasted_iota(jnp.int32, (TOKENS, TOKENS), 1)
    mirrored = (row // 2 % 8) * 16 + (row // 16) * 2 + row % 2
    swap = (mirrored == col).astype(F32)
    swap_bf = swap.astype(BF16)

    def swapped(x):
        return jnp.dot(swap, x, preferred_element_type=F32, precision=lax.Precision.HIGHEST)

    def swapped_bf(x):
        return jnp.dot(swap_bf, x, preferred_element_type=F32).astype(BF16)

    def contract(A, M, first, width):
        def body(i, acc):
            at = pl.multiple_of(i * width, width)
            a = A[:, :, pl.ds(at, width)].reshape(TOKENS, width)
            m = M[:, pl.ds(first + at, width)]
            return acc + lax.dot_general(
                a, m, (((1,), (1,)), ((), ())), preferred_element_type=F32)
        return lax.fori_loop(0, 2, body, jnp.zeros((TOKENS, HID), F32))

    def expand(hidden, out, first, width):
        def body(i, _):
            at = pl.multiple_of(i * width, width)
            y = jnp.dot(hidden, W[:, pl.ds(first + at, width)], preferred_element_type=F32)
            out[:, :, pl.ds(at, width)] = (y * DOWN_SCALE).astype(BF16).reshape(8, ROWS, width)
            return 0
        lax.fori_loop(0, 2, body, 0)

    fly = {}
    RA, RY = v["RA"], v["RY"]

    def rsa_send(w, src, d, s, h):
        fly["a", w, d, s, h] = send(
            src, RA.at[w, d, s, :, colsa(h)], "ra", (w, d, s, h), (g, zring[d]))

    def rsa_start(w, part):
        for d in range(2):
            rsa_send(w, part.at[(z + 4) % NZ, :, colsa(d)], d, 0, d)
        for d in range(2):
            dest = (z + 3) % NZ if d == 0 else (z + NZ - 3) % NZ
            rsa_send(w, part.at[dest, :, colsa(1 - d)], d, 1, 1 - d)

    def rsa_step(w, part, s):
        for h in range(2):
            for d in range(2):
                if ("a", w, d, s - 1, h) not in fly:
                    continue
                fly["a", w, d, s - 1, h].wait_recv()
                dest = (z + 4 - s) % NZ if d == 0 else (z + NZ - 4 + s) % NZ
                held = RA.at[w, d, s - 1, :, colsa(h)]
                held[...] = (
                    held[...].astype(F32) + part[dest, :, colsa(h)].astype(F32)).astype(BF16)
                rsa_send(w, held, d, s, h)

    def rsy_send(w, src, d, k, s, h):
        fly["b", w, d, k, s, h] = send(
            src, RY.at[w, d, k, s, :, colsb(h)], "ry", (w, d, k, s, h), (g, yring[d]))

    def rsb_start(w, part):
        for k in (1, 0):
            for d in range(2):
                rsy_send(w, part.at[slab_of(me, k, 2), :, colsb(d)], d, k, 0, d)
        for k in (1, 0):
            for d in range(2):
                dest = slab_of(me, k, 1 if d == 0 else -1)
                rsy_send(w, part.at[dest, :, colsb(1 - d)], d, k, 1, 1 - d)

    def rsb_step(w, part, k):
        for d in range(2):
            fly["b", w, d, k, 0, d].wait_recv()
            dest = slab_of(me, k, 1 if d == 0 else -1)
            held = RY.at[w, d, k, 0, :, colsb(d)]
            held[...] = (
                held[...].astype(F32) + part[dest, :, colsb(d)].astype(F32)).astype(BF16)
            rsy_send(w, held, d, k, 1, d)

    def rsb_sum(w, part, k, h):
        for d in range(2):
            fly["b", w, d, k, 1, h].wait_recv()
        cols = colsb(h)
        return (
            part[slab_of(me, k, 0), :, cols].astype(F32)
            + RY[w, 0, k, 1, :, cols].astype(F32) + RY[w, 1, k, 1, :, cols].astype(F32))

    def rsb_cross(w, part):
        for h in range(2):
            cols = colsb(h)
            v["XS"][w, :, cols] = rsb_sum(w, part, 1, h).astype(BF16)
            fly["x", w, h] = send(
                v["XS"].at[w, :, cols], v["XR"].at[w, :, cols], "rx", (w, h), (g, flip))

    last = []

    def pieces(w, o, mine, device):
        S, R, stk = v["SP" + o], v["RP" + o], v["STK" + o]
        for j in range(8):
            S[w, j] = stk[2 * j:2 * j + 2, :].astype(BF16)
        for r in range(8):
            if w == 0 and r == 0:
                continue
            to = (mine + r) % 8
            last.append(send(
                S.at[w, to], R.at[w, mine], "p" + o, (w, r), (g if w == 0 else above, device(to))))
        if w == 0:
            R[w, mine] = S[w, mine]

    def rsb_finish(w, part):
        for h in range(2):
            own = rsb_sum(w, part, 0, h)
            fly["x", w, h].wait_recv()
            v["STKb"][:, h * HB:(h + 1) * HB] = own + v["XR"][w, :, colsb(h)].astype(F32)
        pieces(w, "b", z, lambda j: j * NP + me)

    def rsa_finish(w, part):
        for h in range(2):
            for d in range(2):
                fly["a", w, d, 3, h].wait_recv()
        v["STKa"][...] = (
            part[z].astype(F32) + RA[w, 0, 3].astype(F32) + RA[w, 1, 3].astype(F32))
        pieces(w, "a", me, lambda j: base + j)

    pre = (contract(v["Xa"], U, 0, HA) + swapped(contract(v["Xb"], U, CA, HB))) * UP_SCALE
    sig = jax.nn.sigmoid(pre)
    hidden = (pre * sig).astype(BF16)
    hidden_b = swapped_bf(hidden)
    slope = sig * (1.0 + pre * (1.0 - sig))
    expand(hidden, v["P1a"], 0, HA)
    rsa_start(0, v["P1a"])
    expand(hidden_b, v["P1b"], CA, HB)
    rsb_start(0, v["P1b"])
    for c in sent_t:
        c.wait_recv()
    pre_t = (contract(v["Ta"], U, 0, HA) + swapped(contract(v["Tb"], U, CA, HB))) * UP_SCALE
    hidden_t = (pre_t * jax.nn.sigmoid(pre_t)).astype(BF16)
    expand(hidden_t, v["P2a"], 0, HA)
    rsa_start(1, v["P2a"])
    expand(swapped_bf(hidden_t), v["P2b"], CA, HB)
    rsb_start(1, v["P2b"])
    Pa, Pb = (v["P1a"], v["P2a"]), (v["P1b"], v["P2b"])
    rsa_step(0, Pa[0], 1)
    rsb_step(0, Pb[0], 1)
    rsb_step(0, Pb[0], 0)
    rsa_step(1, Pa[1], 1)
    rsb_step(1, Pb[1], 1)
    rsb_step(1, Pb[1], 0)
    rsa_step(0, Pa[0], 2)
    rsb_cross(0, Pb[0])
    rsa_step(1, Pa[1], 2)
    rsb_cross(1, Pb[1])
    rsa_step(0, Pa[0], 3)
    rsb_finish(0, Pb[0])
    rsa_step(1, Pa[1], 3)
    rsb_finish(1, Pb[1])
    rsa_finish(0, Pa[0])
    rsa_finish(1, Pa[1])
    for c in last:
        c.wait_recv()
    for o, first, count in (("a", 0, CA), ("b", CA, CB)):
        ys = jnp.sum(v["RP" + o][0].astype(F32), axis=0)
        yt = jnp.sum(v["RP" + o][1].astype(F32), axis=0)
        goal = v["tgt"][:, first:first + count]
        stu[:, first:first + count] = ys.astype(BF16)
        v["err"][:, first:first + count] = (
            (ys - goal + (ys - yt)) * (1.0 / math.sqrt(TOKENS))).astype(BF16)

    gather(v["err"], "g2", "E", None)

    def downs(rows, E, first, width):
        def body(i, acc):
            at = pl.multiple_of(i * width, width)
            e = E[:, :, pl.ds(at, width)].reshape(TOKENS, width)
            m = W[:, pl.ds(first + at, width)]
            grad = jnp.dot(rows, e, preferred_element_type=F32) * DOWN_SCALE
            W[:, pl.ds(first + at, width)] = (m.astype(F32) - 32.0 * grad).astype(BF16)
            return acc + lax.dot_general(
                e, m, (((1,), (1,)), ((), ())), preferred_element_type=F32)
        return lax.fori_loop(0, 2, body, jnp.zeros((TOKENS, HID), F32))

    def ups(rows, X, first, width):
        def body(i, _):
            at = pl.multiple_of(i * width, width)
            x = X[:, :, pl.ds(at, width)].reshape(TOKENS, width)
            grad = jnp.dot(rows, x, preferred_element_type=F32) * UP_SCALE
            cols = pl.ds(first + at, width)
            U[:, cols] = (U[:, cols].astype(F32) - 32.0 * grad).astype(BF16)
            return 0
        lax.fori_loop(0, 2, body, 0)

    def turned(x):
        return jnp.transpose(x.astype(F32)).astype(BF16)

    back = downs(turned(hidden), v["Ea"], 0, HA) + swapped(downs(turned(hidden_b), v["Eb"], CA, HB))
    store_down = pltpu.make_async_copy(W, ndown_hbm, v["store"].at[0])
    store_down.start()
    dpre = (back * DOWN_SCALE * slope).astype(BF16)
    ups(turned(dpre), v["Xa"], 0, HA)
    ups(turned(swapped_bf(dpre)), v["Xb"], CA, HB)
    store_up = pltpu.make_async_copy(U, nup_hbm, v["store"].at[1])
    store_up.start()
    for c in started:
        c.wait_send()
    store_down.wait()
    store_up.wait()


def shards(tokens, target, up_weight, down_weight):
    anywhere = pl.BlockSpec(memory_space=pl.ANY)
    student, new_up, new_down = pl.pallas_call(
        kernel,
        out_shape=(
            jax.ShapeDtypeStruct((2, D), BF16),
            jax.ShapeDtypeStruct((HID, D), BF16),
            jax.ShapeDtypeStruct((HID, D), BF16),
        ),
        in_specs=[anywhere] * 4,
        out_specs=(pl.BlockSpec(memory_space=pltpu.VMEM), anywhere, anywhere),
        scratch_shapes=list(SCRATCH.values()),
        compiler_params=pltpu.CompilerParams(
            collective_id=0, has_side_effects=True, vmem_limit_bytes=48 * 1024 * 1024),
        cost_estimate=pl.CostEstimate(
            flops=14 * TOKENS * HID * D, bytes_accessed=8 * HID * D, transcendentals=2 * TOKENS * HID),
        name="codistill",
    )(tokens[0], target[0], up_weight[0], down_weight[0])
    return student[None], new_up[None], new_down[None]


def solution(mesh):
    placed = P("group", "fsdp", None)
    return jax.shard_map(
        shards, mesh=mesh, in_specs=(placed,) * 4, out_specs=(placed,) * 3, check_vma=False)
```

time: 1020 us -> 98.2 us (0.10)
  waiting for transfers between devices: 963 us -> 0 us
  Pallas kernels: 0 us -> 90.7 us
  matrix products: 24.8 us -> 0 us
  between operations: 14.4 us -> 0.65 us
    unnamed x4 -> x0, waiting for transfers between devices: 715 us -> none
    all_gather x2 -> x0, waiting for transfers between devices: 248 us -> none  [the longest x1 131 us: shards(): gathered = lax.all_gather(inputs, 'fsdp', axis=0, tiled=True)]
    pallas_call x0 -> x1, Pallas kernels: none -> 90.7 us  [shards(): pl.pallas_call(kernel, out_shape=(jax.ShapeDtypeStruct((2, D), BF16), jax...]
    dot_general x5 -> x0, matrix products: 24.8 us -> none  [the longest x1 7.69 us: teacher_share(): jnp.dot(hidden, lower, preferred_element_type=jnp.float32)]
  transfers between devices with their start and end apart: 5 -> 0, of which waited for: 3 -> 0; matrix products, arithmetic and copies ran while one was open for 1% -> 0% of each run, Pallas kernels for 0% -> 0%
where the time goes in v2:
time: 98.2 us; the launch traced here: 96.3 us
  Pallas kernels  90.7 us (92%)
  local copies, waits for them, and re-layouts  4.94 us (5%)
    pallas_call x1, Pallas kernels, shards(): pl.pallas_call(kernel, out_shape=(jax.ShapeDtypeStruct((2, D), BF16), jax...  90.7 us
    unnamed x7, local copies, waits for them, and re-layouts  4.94 us

profile of v2, /device:TPU:16, one launch (start us, length us, event | category | flops | bytes accessed | tf_op | source)
XLA Modules:
  0.0 96.3 jit_solution(794547464999843290)
XLA Ops:
  0.6 0.0 copy-start
  0.6 0.8 copy-done
  1.5 0.0 copy-start.1
  1.5 0.7 copy-done.1
  2.2 90.7 %codistill.1 = (bf16[2,7168]{1,0:T(2,128)(2,1)S(1)}, bf16[160,7168]{1,0:T(8,128)(2,1)S(1)}, bf16[160,7168]{1,0:T(8,128)(2,1)S(1)}) custom-call(bf16[2,7168]{1,0:T(2,128)(2,1)S(1)} %bitcast.11, f32[2,7168]{1,0:T(2,128)S(1)} %bitcast.10, bf16[160,7168]{1,0:T(8,128)(2,1)} %bitcast.12, bf16[160,7168]{1,0:T(8,128)(2,1)} %bitcast.13), custom_call_target="tpu_custom_call" | custom-call | flops 2055208960 | bytes 9175040 | tf_op jit(solution)/shard_map/codistill/pallas_call | solution.py:427
  92.9 0.6 copy.10
  93.6 1.4 %copy.11 = bf16[1,160,7168]{2,1,0:T(8,128)(2,1)} copy(bf16[1,160,7168]{2,1,0:T(8,128)(2,1)S(1)} %bitcast.8) | data formatting | bytes 4587520
  94.9 1.4 %copy.12 = bf16[1,160,7168]{2,1,0:T(8,128)(2,1)} copy(bf16[1,160,7168]{2,1,0:T(8,128)(2,1)S(1)} %bitcast.7) | data formatting | bytes 4587520
Async XLA Ops:
  0.6 0.8 copy-start
  1.5 0.7 copy-start.1
